TPU v7x, 128 devices: a whole 4x4x4 slice. The times are simulated.
128 devices in a mesh: cluster: 8 (over z, x_hi), dp: 16 (over y, x_lo, core).
Axes of the slice: x: 4 (x_hi: 2, x_lo: 2; x = x_hi * 2 + x_lo), y: 4, z: 4, core: 2. Of those that a mesh axis runs over, the one named last changes fastest.
Arguments:
- documents: bfloat16 [32768, 1024], P('dp', 'cluster'), may hold values from -64 to 64
- centroids: bfloat16 [16384, 1024], P('cluster'), may hold values from -8 to 8
- domain_mass: float32 [32768, 256], P('dp'), may hold values from 0.01 to 10
Outputs:
- lift: float32 [16384, 256], P(('cluster', 'dp'))
- information: float32 [], replicated
All inputs are finite; a program needn't handle non-finite values.
Results may differ from a plain program's by a relative error of at most 0.0013.
Values may be sent and summed in bfloat16 or wider, within the bound.
A program may use at most 128 MiB of HBM per device.

v0:
```python
import math

import jax
import jax.numpy as jnp
from jax import lax
from jax.sharding import PartitionSpec as P

E = 1024


def shards(documents, centroids, domain_mass):
    scale = 3.0 / math.sqrt(E)
    doc_rows = documents.shape[0]
    local_k = centroids.shape[0]
    docs_total = doc_rows * lax.axis_size("dp")
    own_rows = local_k // lax.axis_size("dp")
    columns = centroids
    scores = (
        lax.dot_general(
            lax.all_gather(documents, "cluster", axis=1, tiled=True),
            columns,
            (((1,), (1,)), ((), ())),
            preferred_element_type=jnp.float32,
        )
        * scale
    )
    row_max = lax.pmax(jnp.max(scores, axis=1), "cluster")
    expo = jnp.exp(scores - row_max[:, None])
    row_total = lax.psum(jnp.sum(expo, axis=1), "cluster")
    assign = (expo / row_total[:, None]).astype(jnp.bfloat16)
    shares = (domain_mass / jnp.sum(domain_mass, axis=1, keepdims=True)).astype(jnp.bfloat16)
    columns = assign
    whole = lax.psum(
        lax.dot_general(
            columns, shares, (((0,), (0,)), ((), ())), preferred_element_type=jnp.float32
        ),
        "dp",
    )
    summed = lax.dynamic_slice_in_dim(whole, lax.axis_index("dp") * own_rows, own_rows, 0)
    joint = summed / docs_total
    cluster_mass = jnp.sum(joint, axis=1)
    domain_prior = lax.psum(jnp.sum(joint, axis=0), ("cluster", "dp"))
    lift = joint / (cluster_mass[:, None] * domain_prior[None, :])
    information = lax.psum(jnp.sum(joint * jnp.log(lift)), ("cluster", "dp"))
    return (lift, information)


def solution(mesh):
    return jax.shard_map(
        shards,
        mesh=mesh,
        in_specs=(P("dp", "cluster"), P("cluster", None), P("dp", None)),
        out_specs=(P(("cluster", "dp"), None), P()),
        check_vma=False,
    )
```

profile of v0, /device:TPU:1, one launch (start us, length us, event | category | flops | bytes accessed | tf_op | source)
XLA Modules:
  0.0 423.9 jit_solution(605599507388424641)
XLA Ops:
  7.2 0.0 all-gather.2.cloned.1.call-start
  7.2 0.7 all-gather.2.cloned.1.call-update
  7.9 0.0 all-reduce.2.cloned.1.call-start
  7.9 1.9 reduce_sum.46
  9.9 77.0 %all-gather.2.cloned.1.call-done = bf16[2048,1024]{1,0:T(8,128)(2,1)} async-done(((bf16[2048,128]{1,0:T(8,128)(2,1)}), bf16[2048,1024]{1,0:T(8,128)(2,1)}) %all-gather.2.cloned.1.call-update) | async-done | bytes 4194320 | tf_op jit(solution)/shard_map/all_gather | solution.py:20
  86.9 15.1 %multiply_reduce_fusion = (f32[2048]{0:T(1024)S(1)}, f32[2048,2048]{0,1:T(8,128)}) fusion(bf16[2048,1024]{1,0:T(8,128)(2,1)} %all-gather.2.cloned.1.call-done, bf16[2048,1024]{1,0:T(8,128)(2,1)} %param.4), kind=kOutput, calls=%fused_computation.2 | convolution fusion | flops 8598321152 | bytes 25174016 | tf_op jit(solution)/shard_map/dot_general | solution.py:19
  102.0 16.6 %pmax.7 = f32[2048]{0:T(1024)S(1)} all-reduce(f32[2048]{0:T(1024)S(1)} %get-tuple-element.6), channel_id=1, replica_groups=mesh['cluster'=8,'dp'=16] {'cluster'}, use_global_device_ids=true, to_apply=%region_1.0 | all-reduce | flops 2048 | bytes 16384 | tf_op jit(solution)/shard_map/pmax | solution.py:27
  118.6 0.0 copy-start
  118.6 8.7 %fusion = f32[2048]{0:T(1024)S(1)} fusion(f32[2048,2048]{0,1:T(8,128)} %get-tuple-element.7, f32[2048]{0:T(1024)S(1)} %pmax.7), kind=kLoop, calls=%fused_computation.3 | loop fusion | flops 12580864 | bytes 16793600 | tf_op jit(solution)/shard_map/reduce_sum | solution.py:29
  127.3 18.2 %psum.28 = f32[2048]{0:T(1024)S(1)} all-reduce(f32[2048]{0:T(1024)S(1)} %fusion), channel_id=1, replica_groups=mesh['cluster'=8,'dp'=16] {'cluster'}, use_global_device_ids=true, to_apply=%region_3.0 | all-reduce | flops 2048 | bytes 16384 | tf_op jit(solution)/shard_map/psum | solution.py:29
  145.5 0.0 copy-done
  145.5 9.1 %fusion.1 = f32[2048,256]{1,0:T(8,128)} fusion(f32[2048,2048]{0,1:T(8,128)} %get-tuple-element.7, f32[2048]{0:T(1024)S(1)} %psum.28, f32[2048]{0:T(1024)S(1)} %pmax.7, f32[2048,256]{1,0:T(8,128)S(1)} %copy-done, f32[2048]{0:T(1024)S(1)} %reduce_sum.46), kind=kOutput, calls=%fused_computation.4 | convolution fusion | flops 2165309440 | bytes 20996096 | tf_op jit(solution)/shard_map/dot_general | solution.py:34
  154.6 0.0 all-reduce.2.cloned.1.call-update
  154.7 129.3 %all-reduce.2.cloned.1.call-done = f32[2048,256]{1,0:T(8,128)} async-done(((f32[2048,256]{1,0:T(8,128)}), f32[2048,256]{1,0:T(8,128)}) %all-reduce.2.cloned.1.call-update) | async-done | bytes 2097168 | tf_op jit(solution)/shard_map/psum | solution.py:33
  283.9 1.0 fusion.4
  284.9 67.3 %psum.30 = f32[256]{0:T(256)S(1)} all-reduce(f32[256]{0:T(256)S(1)} %get-tuple-element.3), channel_id=1, replica_groups=mesh['cluster'=8,'dp'=16] {'cluster','dp'}, use_global_device_ids=true, to_apply=%region_8.0 | all-reduce | flops 256 | bytes 2048 | tf_op jit(solution)/shard_map/psum | solution.py:42
  352.2 2.3 multiply_reduce_fusion.1
  354.5 62.6 %psum.31 = f32[]{:T(128)} all-reduce(f32[]{:T(128)} %get-tuple-element.4), channel_id=1, replica_groups=mesh['cluster'=8,'dp'=16] {'cluster','dp'}, use_global_device_ids=true, to_apply=%region_10.0 | all-reduce | flops 1 | bytes 8 | tf_op jit(solution)/shard_map/psum | solution.py:44
Async XLA Ops:
  7.2 79.7 %all-gather.2.cloned.1.call-start = ((), (), s32[]{:S(2)}) async-start(), calls=%async_computation | async-start | bytes 4718592 | tf_op jit(solution)/shard_map/all_gather | solution.py:20
  7.9 276.0 %all-reduce.2.cloned.1.call-start = ((), (), s32[]{:S(2)}) async-start(), calls=%async_computation.1 | async-start | bytes 4194304 | tf_op jit(solution)/shard_map/psum | solution.py:33
  118.6 26.9 %copy-start = (f32[2048,256]{1,0:T(8,128)S(1)}, f32[2048,256]{1,0:T(8,128)}, u32[]{:S(2)}) copy-start(f32[2048,256]{1,0:T(8,128)} %param.5) | copy-start | bytes 6291460
Sparse Core Ops, SparseCore 0:
  10.2 76.6 all-gather.1
  154.8 129.0 all-reduce.1
where the time goes:
time: 424 us
  waiting for transfers between devices  207 us (49%)
  blocking collectives  165 us (39%)
  matrix products  24.2 us (6%)
  between operations  14.1 us (3%)
  other arithmetic  13.9 us (3%)
    psum x1, waiting for transfers between devices, shards(): lax.psum(lax.dot_general(columns, shares, (((0,), (0,)), ((), ())), prefe...  129 us
    all_gather x1, waiting for transfers between devices, shards(): lax.all_gather(documents, 'cluster', axis=1, tiled=True)  77 us
    psum x1, blocking collectives, shards(): domain_prior = lax.psum(jnp.sum(joint, axis=0), ('cluster', 'dp'))  67.3 us
    psum x1, blocking collectives, shards(): information = lax.psum(jnp.sum(joint * jnp.log(lift)), ('cluster', 'dp'))  62.6 us
    psum x1, blocking collectives, shards(): row_total = lax.psum(jnp.sum(expo, axis=1), 'cluster')  18.2 us
    pmax x1, blocking collectives, shards(): row_max = lax.pmax(jnp.max(scores, axis=1), 'cluster')  16.6 us
    dot_general x1, matrix products, shards(): lax.dot_general(lax.all_gather(documents, 'cluster', axis=1, tiled=True),...  15.1 us
    dot_general x1, matrix products, shards(): lax.dot_general(columns, shares, (((0,), (0,)), ((), ())), preferred_elem...  9.11 us
  transfers between devices with their start and end apart: 2, of which 2 were waited for; matrix products, arithmetic and copies ran while one was open for 0% of the time, Pallas kernels for 0%

commit v1 on v0

v1 whole, which is shorter than its diff:
```python
import math

import jax
import jax.numpy as jnp
from jax import lax
from jax.experimental import pallas as pl
from jax.experimental.pallas import tpu as pltpu
from jax.sharding import PartitionSpec as P

MESH = pl.DeviceIdType.MESH
NT = (((1,), (1,)), ((), ()))

E = 1024
G = 256
DOCS = 32768
HALF = 1024
CH = 256
NJ = HALF // CH
NU = 2 * NJ
STRIPE = 128
ROWS = 1024
EXP2_SCALE = 3.0 / math.sqrt(E) * math.log2(math.e)
REL_Y = (0, 1, 3, 2)
SLOT = {rel: p for p, rel in enumerate(REL_Y)}
SETS = ((0, 1024), (1024, 768), (1792, 256))


def kernel(docs_hbm, cent_hbm, mass_hbm, lift_ref, info_ref,
           docs, own_c, far_c, mass, shares, expo, setstat, stats, acc,
           rs_out, rs_in, pr_out, pr_in, pr2_out, pr2_in, in_out, in_in, in2_out, in2_in,
           load_sem, x_send, x_recv, z_send, z_recv, f_send, f_recv, s_send, s_recv,
           b_send, b_recv, y_send, y_recv, h_send, h_recv, st_send, st_recv,
           rs_send, rs_recv, pr_send, pr_recv, pr2_send, pr2_recv, in_send, in_recv, in2_send, in2_recv):
    c = lax.axis_index("cluster")
    d = lax.axis_index("dp")
    z, xh = c // 2, lax.rem(c, 2)
    y, xl, q = d // 4, lax.rem(d // 2, 2), lax.rem(d, 2)

    def dev(dz=0, fx=0, dy=0, fl=0, fq=0):
        zz = lax.rem(z + dz, 4) if dz else z
        yy = lax.rem(y + dy, 4) if dy else y
        hh = 1 - xh if fx else xh
        ll = 1 - xl if fl else xl
        qq = 1 - q if fq else q
        return (zz * 2 + hh, (yy * 2 + ll) * 2 + qq)

    line = [(dz, fq) for fq in (0, 1) for dz in (0, 1, 2, 3) if dz or fq]
    plane = [(fx, dy, fl) for fx in (0, 1) for dy in (0, 1, 2, 3) for fl in (0, 1) if fx or dy or fl]

    def remote(src, dst, send, recv, device):
        return pltpu.make_async_remote_copy(
            src_ref=src, dst_ref=dst, send_sem=send, recv_sem=recv,
            device_id=device, device_id_type=MESH)

    barrier = pltpu.get_barrier_semaphore()
    for dz, fq in line:
        pl.semaphore_signal(barrier, inc=1, device_id=dev(dz=dz, fq=fq), device_id_type=MESH)
    for fx, dy, fl in plane:
        pl.semaphore_signal(barrier, inc=1, device_id=dev(fx=fx, dy=dy, fl=fl), device_id_type=MESH)

    def cols(cc):
        return pl.ds(pl.multiple_of(cc * 128, 128), 128)

    mine, other = cols(c), cols(z * 2 + 1 - xh)
    base = xh * HALF

    loads = [pltpu.make_async_copy(mass_hbm.at[pl.ds(pl.multiple_of(base, HALF), HALF)], mass, load_sem.at[0])]
    for j in range(NJ):
        rows = pl.ds(pl.multiple_of(base + j * CH, CH), CH)
        loads.append(pltpu.make_async_copy(docs_hbm.at[rows], docs.at[2 * j, :, mine], load_sem.at[1 + j]))
    for p in range(4):
        for fl in range(2):
            u = lax.rem(y + REL_Y[p], 4) * 2 + (1 - xl if fl else xl)
            row = pl.multiple_of(u * 256 + q * STRIPE, STRIPE)
            k = p * 2 + fl
            loads.append(pltpu.make_async_copy(
                cent_hbm.at[pl.ds(row, STRIPE)], own_c.at[pl.ds(k * STRIPE, STRIPE)], load_sem.at[1 + NJ + k]))
    for copy in loads:
        copy.start()
    loads[0].wait()
    pl.semaphore_wait(barrier, len(line) + len(plane))

    sends = []

    def go(copy):
        copy.start()
        sends.append(copy)
        return copy

    x_copies = []
    for j in range(NJ):
        rows = pl.ds(pl.multiple_of((1 - xh) * HALF + j * CH, CH), CH)
        x_copies.append(go(remote(docs_hbm.at[rows], docs.at[2 * j, :, mine], x_send.at[j], x_recv.at[j], dev(fx=1))))
    b_copies = []
    for fl in range(2):
        u = y * 2 + (xl if fl else 1 - xl)
        row = pl.multiple_of(u * 256 + q * STRIPE, STRIPE)
        b_copies.append(go(remote(
            cent_hbm.at[pl.ds(row, STRIPE)], far_c.at[pl.ds(fl * STRIPE, STRIPE)],
            b_send.at[fl], b_recv.at[fl], dev(fx=1, fl=1))))
    z_copies = []
    for j in range(NJ):
        rows = pl.ds(pl.multiple_of(base + j * CH, CH), CH)
        for dz in (1, 3, 2):
            z_copies.append(go(remote(
                docs_hbm.at[rows], docs.at[2 * j, :, mine], z_send.at[j, dz - 1], z_recv.at[j, dz - 1], dev(dz=dz))))

    for r in range(0, HALF, 256):
        block = mass[r:r + 256]
        shares[0, r:r + 256] = (block / jnp.sum(block, axis=1, keepdims=True)).astype(jnp.bfloat16)
    h_copy = go(remote(shares.at[0], shares.at[1], h_send, h_recv, dev(fq=1)))

    f_copies, y_copies = [], []

    def forward_x(j):
        x_copies[j].wait_recv()
        for dz in (1, 3, 2):
            f_copies.append(go(remote(
                docs.at[2 * j, :, other], docs.at[2 * j, :, other],
                f_send.at[j, dz - 1], f_recv.at[j, dz - 1], dev(dz=dz))))

    def forward_b(fl):
        b_copies[fl].wait_recv()
        for dy in (1, 3, 2):
            k = SLOT[4 - dy] * 2 + fl
            y_copies.append(go(remote(
                far_c.at[pl.ds(fl * STRIPE, STRIPE)], far_c.at[pl.ds(k * STRIPE, STRIPE)],
                y_send.at[fl, dy - 1], y_recv.at[fl, dy - 1], dev(dy=dy))))

    forward_x(0)
    forward_x(1)
    forward_b(0)
    forward_x(2)
    forward_x(3)
    forward_b(1)

    def part(u, s):
        start, count = SETS[s]
        block_docs = docs[u]
        top = jnp.full((8, CH), -jnp.inf, jnp.float32)
        for r in range(start, start + count, 256):
            block = own_c[r:r + 256] if r < ROWS else far_c[r - ROWS:r - ROWS + 256]
            raw = lax.dot_general(block, block_docs, NT, preferred_element_type=jnp.float32)
            expo[u, r:r + 256] = raw
            top = jnp.maximum(top, jnp.max(raw.reshape(32, 8, CH), axis=0))
        top = jnp.max(top, axis=0, keepdims=True)
        total = jnp.zeros((8, CH), jnp.float32)
        for r in range(start, start + count, 256):
            value = jnp.exp2((expo[u, r:r + 256] - top) * EXP2_SCALE)
            expo[u, r:r + 256] = value
            total = total + jnp.sum(value.reshape(32, 8, CH), axis=0)
        setstat[u, s:s + 1] = top
        setstat[u, 3 + s:4 + s] = jnp.sum(total, axis=0, keepdims=True)

    s_copies = []

    def gather_chunk(j):
        loads[1 + j].wait()
        for dz in (1, 3, 2):
            z_copies[3 * j + (1, 3, 2).index(dz)].wait_recv()
            f_copies[3 * j + (1, 3, 2).index(dz)].wait_recv()
        s_copies.append(go(remote(docs.at[2 * j], docs.at[2 * j + 1], s_send.at[j], s_recv.at[j], dev(fq=1))))

    for j in range(NJ - 1):
        gather_chunk(j)
        if j == 0:
            for copy in loads[1 + NJ:]:
                copy.wait()
        part(2 * j, 0)
        s_copies[j].wait_recv()
        part(2 * j + 1, 0)

    for i in (0, 1, 3, 4):
        y_copies[i].wait_recv()

    @pl.loop(0, NU - 2)
    def _(u):
        part(u, 1)

    gather_chunk(NJ - 1)
    part(NU - 2, 0)
    part(NU - 2, 1)
    s_copies[NJ - 1].wait_recv()
    part(NU - 1, 0)
    part(NU - 1, 1)
    for copy in y_copies[2::3]:
        copy.wait_recv()

    me = z * 2 + q

    def stat_copy(u, i):
        dz, fq = line[i]
        there = u + 1 - 2 * lax.rem(u, 2) if fq else u
        return remote(stats.at[u, me], stats.at[there, me], st_send.at[u, i], st_recv.at[there, i], dev(dz=dz, fq=fq))

    @pl.loop(0, NU)
    def _(u):
        part(u, 2)
        top3 = setstat[u, 0:3]
        top = jnp.max(top3, axis=0, keepdims=True)
        total = jnp.sum(setstat[u, 3:6] * jnp.exp2((top3 - top) * EXP2_SCALE), axis=0, keepdims=True)
        stats[u, me, 0:1] = top
        stats[u, me, 1:2] = total
        for i in range(len(line)):
            stat_copy(u, i).start()

    h_copy.wait_recv()

    @pl.loop(0, NU)
    def _(u):
        for i in range(len(line)):
            stat_copy(u, i).wait_send()
        for i in range(len(line)):
            dz, fq = line[i]
            remote(stats.at[u, me], stats.at[u, me], st_send.at[u, i], st_recv.at[u, i], dev(dz=dz, fq=fq)).wait_recv()
        tops = stats[u, :, 0, :]
        totals = stats[u, :, 1, :]
        top = jnp.max(tops, axis=0, keepdims=True)
        total = jnp.sum(totals * jnp.exp2((tops - top) * EXP2_SCALE), axis=0, keepdims=True)
        factor = jnp.exp2((setstat[u, 0:3] - top) * EXP2_SCALE) / total
        block_shares = shares[lax.rem(u, 2), pl.ds(pl.multiple_of(u // 2 * CH, CH), CH)]
        first = u == 0
        for s, (start, count) in enumerate(SETS):
            for r in range(start, start + count, 256):
                assign = (expo[u, r:r + 256] * factor[s:s + 1]).astype(jnp.bfloat16)
                term = jnp.dot(assign, block_shares, preferred_element_type=jnp.float32)
                acc[r:r + 256] = jnp.where(first, term, acc[r:r + 256] + term)

    rs_copies = []
    for k in range(1, 16):
        fx, p, fl = k // 8, k // 2 % 4, k % 2
        rows = pl.ds(k * STRIPE, STRIPE)
        rs_out[rows] = acc[rows].astype(jnp.bfloat16)
        rs_copies.append(go(remote(
            rs_out.at[rows], rs_in.at[k], rs_send.at[k], rs_recv.at[k], dev(fx=fx, dy=REL_Y[p], fl=fl))))

    here = (y * 2 + xl) * 2 + xh
    column = jnp.zeros((8, G), jnp.float32)
    for r in range(0, 2 * ROWS, 256):
        column = column + jnp.sum(acc[r:r + 256].reshape(32, 8, G), axis=0)

    def reduce_over(value, peers, index, out, box, send, recv):
        out[...] = value
        box[index] = value
        copies = [go(remote(out, box.at[index], send.at[i], recv.at[i], peer)) for i, peer in enumerate(peers)]
        return copies

    plane_devices = [dev(fx=fx, dy=dy, fl=fl) for fx, dy, fl in plane]
    line_devices = [dev(dz=dz, fq=fq) for dz, fq in line]
    copies = reduce_over(jnp.sum(column, axis=0, keepdims=True), plane_devices, here, pr_out, pr_in, pr_send, pr_recv)
    for copy in copies:
        copy.wait_recv()
    copies = reduce_over(jnp.sum(pr_in[...], axis=0), line_devices, me, pr2_out, pr2_in, pr2_send, pr2_recv)

    total = acc[0:STRIPE]
    for k, copy in enumerate(rs_copies):
        copy.wait_recv()
        total = total + rs_in[k + 1].astype(jnp.float32)
    for copy in copies:
        copy.wait_recv()
    prior = jnp.sum(pr2_in[...], axis=0) / DOCS
    joint = total / DOCS
    cluster_mass = jnp.sum(joint, axis=1, keepdims=True)
    lift = joint / (cluster_mass * prior)
    lift_ref[...] = lift
    information = jnp.sum((joint * jnp.log(lift)).reshape(STRIPE // 8, 8, G), axis=0)
    information = jnp.sum(information, axis=0, keepdims=True)

    copies = reduce_over(information, line_devices, me, in_out, in_in, in_send, in_recv)
    for copy in copies:
        copy.wait_recv()
    copies = reduce_over(jnp.sum(in_in[...], axis=0), plane_devices, here, in2_out, in2_in, in2_send, in2_recv)
    for copy in copies:
        copy.wait_recv()
    info_ref[...] = jnp.sum(jnp.sum(in2_in[...], axis=0), axis=1, keepdims=True)
    for copy in sends:
        copy.wait_send()


def shards(documents, centroids, domain_mass):
    bf16, f32 = jnp.bfloat16, jnp.float32
    dma = pltpu.SemaphoreType.DMA
    vmem = pltpu.VMEM
    lift, information = pl.pallas_call(
        kernel,
        out_shape=(jax.ShapeDtypeStruct((STRIPE, G), f32), jax.ShapeDtypeStruct((1, 1), f32)),
        in_specs=[pl.BlockSpec(memory_space=pl.ANY)] * 3,
        out_specs=(pl.BlockSpec(memory_space=pltpu.VMEM), pl.BlockSpec(memory_space=pltpu.VMEM)),
        scratch_shapes=[
            vmem((NU, CH, E), bf16),
            vmem((ROWS, E), bf16),
            vmem((ROWS, E), bf16),
            vmem((HALF, G), f32),
            vmem((2, HALF, G), bf16),
            vmem((NU, 2 * ROWS, CH), f32),
            vmem((NU, 8, CH), f32),
            vmem((NU, 8, 2, CH), f32),
            vmem((2 * ROWS, G), f32),
            vmem((2 * ROWS, G), bf16),
            vmem((16, STRIPE, G), bf16),
            vmem((1, G), f32),
            vmem((16, 1, G), f32),
            vmem((1, G), f32),
            vmem((8, 1, G), f32),
            vmem((1, G), f32),
            vmem((8, 1, G), f32),
            vmem((1, G), f32),
            vmem((16, 1, G), f32),
            dma((1 + NJ + 8,)),
            dma((NJ,)), dma((NJ,)),
            dma((NJ, 3)), dma((NJ, 3)),
            dma((NJ, 3)), dma((NJ, 3)),
            dma((NJ,)), dma((NJ,)),
            dma((2,)), dma((2,)),
            dma((2, 3)), dma((2, 3)),
            dma, dma,
            dma((NU, 7)), dma((NU, 7)),
            dma((16,)), dma((16,)),
            dma((15,)), dma((15,)),
            dma((7,)), dma((7,)),
            dma((7,)), dma((7,)),
            dma((15,)), dma((15,)),
        ],
        compiler_params=pltpu.CompilerParams(
            collective_id=0, has_side_effects=True, vmem_limit_bytes=56 << 20),
    )(documents, centroids, domain_mass)
    return lift, information.reshape(())


def solution(mesh):
    return jax.shard_map(
        shards,
        mesh=mesh,
        in_specs=(P("dp", "cluster"), P("cluster", None), P("dp", None)),
        out_specs=(P(("cluster", "dp"), None), P()),
        check_vma=False,
    )
```

time: 424 us -> 94.3 us (0.22)
  waiting for transfers between devices: 207 us -> 0 us
  blocking collectives: 165 us -> 0 us
  Pallas kernels: 0 us -> 90.1 us
  matrix products: 24.2 us -> 0 us
  other arithmetic: 13.9 us -> 0 us
  between operations: 14.1 us -> 2.45 us
    psum x3 -> x0, blocking collectives: 148 us -> none  [the longest x1 67.3 us: shards(): domain_prior = lax.psum(jnp.sum(joint, axis=0), ('cluster', 'dp'))]
    psum x1 -> x0, waiting for transfers between devices: 129 us -> none  [shards(): lax.psum(lax.dot_general(columns, shares, (((0,), (0,)), ((), ())), prefe...]
    pallas_call x0 -> x1, Pallas kernels: none -> 90.1 us  [shards(): pl.pallas_call(kernel, out_shape=(jax.ShapeDtypeStruct((STRIPE, G), f32),...]
    all_gather x1 -> x0, waiting for transfers between devices: 77 us -> none  [shards(): lax.all_gather(documents, 'cluster', axis=1, tiled=True)]
    dot_general x2 -> x0, matrix products: 24.2 us -> none  [the longest x1 15.1 us: shards(): lax.dot_general(lax.all_gather(documents, 'cluster', axis=1, tiled=True),...]
    pmax x1 -> x0, blocking collectives: 16.6 us -> none  [shards(): row_max = lax.pmax(jnp.max(scores, axis=1), 'cluster')]
    reduce_sum x4 -> x0, other arithmetic: 13.9 us -> none  [the longest x1 8.7 us: shards(): row_total = lax.psum(jnp.sum(expo, axis=1), 'cluster')]
  transfers between devices with their start and end apart: 2 -> 0, of which waited for: 2 -> 0; matrix products, arithmetic and copies ran while one was open for 0% -> 0% of each run, Pallas kernels for 0% -> 0%
where the time goes in v1:
time: 94.3 us; the launch traced here: 94.1 us
  Pallas kernels  90.1 us (96%)
  between operations  2.45 us (3%)
  local copies, waits for them, and re-layouts  1.57 us (2%)
    pallas_call x1, Pallas kernels, shards(): pl.pallas_call(kernel, out_shape=(jax.ShapeDtypeStruct((STRIPE, G), f32),...  90.1 us

profile of v1, /device:TPU:1, one launch (start us, length us, event | category | flops | bytes accessed | tf_op | source)
XLA Modules:
  0.0 94.1 jit_solution(4395744626557694733)
XLA Ops:
  0.6 90.1 %shard_map.50 = (f32[128,256]{1,0:T(8,128)}, f32[1,1]{1,0:T(1,128)}) custom-call(bf16[2048,128]{1,0:T(8,128)(2,1)} %docs_hbm.1, bf16[2048,1024]{1,0:T(8,128)(2,1)} %cent_hbm.1, f32[2048,256]{1,0:T(8,128)} %mass_hbm.1), custom_call_target="tpu_custom_call" | custom-call | tf_op jit(solution)/shard_map/pallas_call | solution.py:284
  90.7 1.6 %copy.7 = f32[128,256]{1,0:T(8,128)} copy(f32[128,256]{1,0:T(8,128)} %get-tuple-element.8) | data formatting | bytes 262144

commit v2 on v1

v2 whole, which is shorter than its diff:
```python
import math

import jax
import jax.numpy as jnp
from jax import lax
from jax.experimental import pallas as pl
from jax.experimental.pallas import tpu as pltpu
from jax.sharding import PartitionSpec as P

MESH = pl.DeviceIdType.MESH
NT = (((1,), (1,)), ((), ()))

E = 1024
G = 256
DOCS = 32768
HALF = 1024
CH = 256
NJ = HALF // CH
NB = 8
PIECE = 256 // NB
DIRECT = (0, 1, 2, 3, 4, 5, 6, 7)
WAYS = (1, 3, 2)
ZN, FN, ZW = 2, 3, 4
PRIOR_FIRST = True
SCHEDULE = (
    "x0", "b0", "z0", "x1", "b1", "z1", "x2", "b2", "z2", "x3", "b3", "z3",
    "l0", "D0,1,2,3,4,5,6,7", "l1", "L", "c0", "l2", "l3", "p0,0", "s0", "p1,0", "c1", "p2,0",
    "s1", "p3,0", "a0,4", "P0,4,1", "c2", "a4,8", "P0,4,2", "P0,4,3", "w4", "s2", "c3", "w5",
    "t0", "w6", "s3", "w7", "t1",
)
XW, BW = 4, 4
BATCHES = ((0, 6), (6, 8))
EARLY = 6
ORDER = (14, 6, 15, 7, 10, 2, 11, 3, 12, 4, 13, 5, 8, 1, 9, 0)
NU = 2 * NJ
STRIPE = 128
ROWS = 1024
EXP2_SCALE = 3.0 / math.sqrt(E) * math.log2(math.e)
REL_Y = (0, 1, 3, 2)
SLOT = {rel: p for p, rel in enumerate(REL_Y)}
SETS = ((0, 1024), (1024, 512), (1536, 256), (1792, 256))
NS = len(SETS)


def kernel(docs_hbm, cent_hbm, mass_hbm, lift_ref, info_ref,
           docs, own_c, far_c, mass, shares, expo, setstat, stats, acc,
           rs_out, rs_in, pr_out, pr_in, pr2_out, pr2_in, in_out, in_in, in2_out, in2_in,
           load_sem, x_send, x_recv, z_send, z_recv, zz_send, zz_recv, f_send, f_recv, ff_send, ff_recv, s_send, s_recv,
           b_send, b_recv, l_send, l_recv, y_send, y_recv, h_send, h_recv, st_send, st_recv,
           rs_send, rs_recv, pr_send, pr_recv, pr2_send, pr2_recv, in_send, in_recv, in2_send, in2_recv):
    c = lax.axis_index("cluster")
    d = lax.axis_index("dp")
    z, xh = c // 2, lax.rem(c, 2)
    y, xl, q = d // 4, lax.rem(d // 2, 2), lax.rem(d, 2)

    def dev(dz=0, fx=0, dy=0, fl=0, fq=0):
        zz = lax.rem(z + dz, 4) if dz else z
        yy = lax.rem(y + dy, 4) if dy else y
        hh = 1 - xh if fx else xh
        ll = 1 - xl if fl else xl
        qq = 1 - q if fq else q
        return (zz * 2 + hh, (yy * 2 + ll) * 2 + qq)

    line = [(dz, fq) for fq in (0, 1) for dz in (0, 1, 2, 3) if dz or fq]
    plane = [(fx, dy, fl) for fx in (0, 1) for dy in (0, 1, 2, 3) for fl in (0, 1) if fx or dy or fl]

    def remote(src, dst, send, recv, device):
        return pltpu.make_async_remote_copy(
            src_ref=src, dst_ref=dst, send_sem=send, recv_sem=recv,
            device_id=device, device_id_type=MESH)

    barrier = pltpu.get_barrier_semaphore()
    for dz, fq in line:
        pl.semaphore_signal(barrier, inc=1, device_id=dev(dz=dz, fq=fq), device_id_type=MESH)
    for fx, dy, fl in plane:
        pl.semaphore_signal(barrier, inc=1, device_id=dev(fx=fx, dy=dy, fl=fl), device_id_type=MESH)

    def cols(cc):
        return pl.ds(pl.multiple_of(cc * 128, 128), 128)

    mine, other = cols(c), cols(z * 2 + 1 - xh)
    base = xh * HALF

    loads = [pltpu.make_async_copy(mass_hbm.at[pl.ds(pl.multiple_of(base, HALF), HALF)], mass, load_sem.at[0])]
    for j in range(NJ):
        rows = pl.ds(pl.multiple_of(base + j * CH, CH), CH)
        loads.append(pltpu.make_async_copy(docs_hbm.at[rows], docs.at[2 * j, :, mine], load_sem.at[1 + j]))
    for p in range(4):
        for fl in range(2):
            u = lax.rem(y + REL_Y[p], 4) * 2 + (1 - xl if fl else xl)
            row = pl.multiple_of(u * 256 + q * STRIPE, STRIPE)
            k = p * 2 + fl
            loads.append(pltpu.make_async_copy(
                cent_hbm.at[pl.ds(row, STRIPE)], own_c.at[pl.ds(k * STRIPE, STRIPE)], load_sem.at[1 + NJ + k]))
    for copy in loads:
        copy.start()
    loads[0].wait()
    pl.semaphore_wait(barrier, len(line) + len(plane))

    sends = []

    def go(copy):
        copy.start()
        sends.append(copy)
        return copy

    x_copies = []
    for j in range(NJ):
        rows = pl.ds(pl.multiple_of((1 - xh) * HALF + j * CH, CH), CH)
        x_copies.append(remote(docs_hbm.at[rows], docs.at[2 * j, :, mine], x_send.at[j], x_recv.at[j], dev(fx=1)))

    def far(n, p):
        return far_c.at[pl.ds((4 * n + p) * PIECE, PIECE)]

    def cross(n, dy, sem):
        flip = n % 2
        u = lax.rem(y + dy, 4) * 2 + (xl if flip else 1 - xl)
        row = pl.multiple_of(u * 256 + q * STRIPE + n // 2 * PIECE, PIECE)
        return remote(cent_hbm.at[pl.ds(row, PIECE)], far(n, SLOT[dy]), b_send.at[sem], b_recv.at[sem], dev(fx=1, fl=1))

    b_copies = [cross(2 * i, 0, i) for i in range(NB // 2)]
    d_copies = {n: cross(n, 2, NB // 2 + n) for n in DIRECT}

    z_copies = []
    for j in range(NJ):
        rows = pl.ds(pl.multiple_of(base + j * CH, CH), CH)
        z_copies.append([remote(
            docs_hbm.at[rows], docs.at[2 * j, :, mine], z_send.at[j, i], z_recv.at[j, i], dev(dz=WAYS[i]))
            for i in range(ZN)])

    def send_z(j):
        for copy in z_copies[j]:
            go(copy)

    def send_d(*pieces):
        for n in pieces:
            go(d_copies[n])

    for copy in x_copies[:XW]:
        go(copy)
    for copy in b_copies[:BW]:
        go(copy)
    for j in range(ZW):
        send_z(j)

    for r in range(0, HALF, 256):
        block = mass[r:r + 256]
        shares[0, r:r + 256] = (block / jnp.sum(block, axis=1, keepdims=True)).astype(jnp.bfloat16)
    h_copy = go(remote(shares.at[0], shares.at[1], h_send, h_recv, dev(fq=1)))

    f_copies, y_copies, l_copies = [], {}, []
    zz_copies, ff_copies = {}, {}

    def arrive_x(j):
        x_copies[j].wait_recv()
        if j + XW < NJ:
            go(x_copies[j + XW])
        f_copies.append([go(remote(
            docs.at[2 * j, :, other], docs.at[2 * j, :, other],
            f_send.at[j, i], f_recv.at[j, i], dev(dz=WAYS[i]))) for i in range(FN)])

    def pass_on(j, copies, side, send, recv, out):
        for i in range(2):
            copies[j][i].wait_recv()
            column = cols(lax.rem(z + (3, 1)[i], 4) * 2 + side)
            part_docs = docs.at[2 * j, pl.ds(i * CH // 2, CH // 2), column]
            out[j, i] = go(remote(part_docs, part_docs, send.at[j, i], recv.at[j, i], dev(dz=(1, 3)[i])))

    def arrive_z(j):
        pass_on(j, z_copies, xh, zz_send, zz_recv, zz_copies)

    def arrive_f(j):
        pass_on(j, f_copies, 1 - xh, ff_send, ff_recv, ff_copies)

    def along_y(n):
        y_copies[n] = [go(remote(far(n, 0), far(n, SLOT[4 - dy]), y_send.at[n, dy - 1], y_recv.at[n, dy - 1], dev(dy=dy)))
                       for dy in ((1, 3) if n in DIRECT else (1, 3, 2))]

    def arrive_b(i):
        b_copies[i].wait_recv()
        if i + BW < NB // 2:
            go(b_copies[i + BW])
        l_copies.append(go(remote(far(2 * i, 0), far(2 * i + 1, 0), l_send.at[i], l_recv.at[i], dev(fl=1))))
        along_y(2 * i)

    def arrive_l(i):
        l_copies[i].wait_recv()
        along_y(2 * i + 1)

    def part(u, s):
        start, count = SETS[s] if s is not None else (0, 2 * ROWS)
        block_docs = docs[u]
        top = jnp.full((8, CH), -jnp.inf, jnp.float32)
        for r in range(start, start + count, 256):
            block = own_c[r:r + 256] if r < ROWS else far_c[r - ROWS:r - ROWS + 256]
            raw = lax.dot_general(block, block_docs, NT, preferred_element_type=jnp.float32)
            expo[u, r:r + 256] = raw
            top = jnp.maximum(top, jnp.max(raw.reshape(32, 8, CH), axis=0))
        top = jnp.max(top, axis=0, keepdims=True)
        total = jnp.zeros((8, CH), jnp.float32)
        for r in range(start, start + count, 256):
            value = jnp.exp2((expo[u, r:r + 256] - top) * EXP2_SCALE)
            expo[u, r:r + 256] = value
            total = total + jnp.sum(value.reshape(32, 8, CH), axis=0)
        total = jnp.sum(total, axis=0, keepdims=True)
        if s is None:
            setstat[u, 0:NS] = jnp.broadcast_to(top, (NS, CH))
            setstat[u, NS:2 * NS] = jnp.concatenate([total, jnp.zeros((NS - 1, CH), jnp.float32)], axis=0)
        else:
            setstat[u, s:s + 1] = top
            setstat[u, NS + s:NS + s + 1] = total

    s_copies = []

    def gather_chunk(j):
        loads[1 + j].wait()
        for i in range(2):
            if ZN == 2:
                zz_copies[j, i].wait_recv()
            if FN == 2:
                ff_copies[j, i].wait_recv()
        for copies in (z_copies[j] if ZN == 3 else []) + (f_copies[j] if FN == 3 else []):
            copies.wait_recv()
        s_copies.append(go(remote(docs.at[2 * j], docs.at[2 * j + 1], s_send.at[j], s_recv.at[j], dev(fq=1))))

    def gather_sibling(j):
        s_copies[j].wait_recv()

    def far_pieces(first, last):
        for n in range(first, last):
            for copy in y_copies[n]:
                copy.wait_recv()
            if n in DIRECT:
                d_copies[n].wait_recv()

    me = z * 2 + q

    def group_unit(u):
        return u + q * (1 - 2 * lax.rem(u, 2))

    def merge(u):
        top_set = setstat[u, 0:NS]
        top = jnp.max(top_set, axis=0, keepdims=True)
        total = jnp.sum(setstat[u, NS:2 * NS] * jnp.exp2((top_set - top) * EXP2_SCALE), axis=0, keepdims=True)
        stats[me, group_unit(u), 0:1] = top
        stats[me, group_unit(u), 1:2] = total

    st_copies = {}

    def send_stats(batch):
        first, last = BATCHES[batch]

        @pl.loop(first, last)
        def _(u):
            merge(u)
        block = stats.at[me, pl.ds(first, last - first)]
        st_copies[batch] = [go(remote(block, block, st_send.at[batch, i], st_recv.at[batch, i], dev(dz=dz, fq=fq)))
                            for i, (dz, fq) in enumerate(line)]

    def whole(u):
        part(u, None)

    def loaded():
        for copy in loads[1 + NJ:]:
            copy.wait()

    def parts(first, last, s):
        @pl.loop(first, last)
        def _(u):
            part(u, s)

    steps = {"b": arrive_b, "x": arrive_x, "z": arrive_z, "f": arrive_f, "l": arrive_l, "c": gather_chunk, "s": gather_sibling,
             "Z": send_z, "D": send_d, "L": loaded, "p": part, "P": parts, "a": far_pieces, "w": whole, "t": send_stats}
    for step in SCHEDULE:
        steps[step[0]](*[int(v) for v in step[1:].split(",") if v])

    def factors(batch):
        for copy in st_copies[batch]:
            copy.wait_recv()

        @pl.loop(*BATCHES[batch])
        def _(u):
            tops = stats[:, group_unit(u), 0, :]
            totals = stats[:, group_unit(u), 1, :]
            top = jnp.max(tops, axis=0, keepdims=True)
            total = jnp.sum(totals * jnp.exp2((tops - top) * EXP2_SCALE), axis=0, keepdims=True)
            setstat[u, 0:NS] = jnp.exp2((setstat[u, 0:NS] - top) * EXP2_SCALE) / total

    def product(k, u):
        if k < 8:
            assign = expo[u, k * STRIPE:(k + 1) * STRIPE] * setstat[u, 0:1]
        else:
            p, fl = k // 2 % 4, k % 2
            rows = []
            for i in range(fl, NB, 2):
                r = ROWS + (4 * i + p) * PIECE
                s = [n for n, (start, count) in enumerate(SETS) if start <= r < start + count][0]
                rows.append(expo[u, r:r + PIECE] * setstat[u, s:s + 1])
            assign = jnp.concatenate(rows, axis=0)
        return jnp.dot(assign.astype(jnp.bfloat16), shares[u % 2, u // 2 * CH:(u // 2 + 1) * CH],
                       preferred_element_type=jnp.float32)

    h_copy.wait_recv()
    factors(0)

    for k in range(16):
        joint = product(k, 0)
        for u in range(1, EARLY):
            joint = joint + product(k, u)
        acc[k * STRIPE:(k + 1) * STRIPE] = joint

    factors(1)

    rs_copies = {}
    column = jnp.zeros((8, G), jnp.float32)
    for k in ORDER:
        rows = pl.ds(k * STRIPE, STRIPE)
        joint = acc[rows]
        for u in range(EARLY, NU):
            joint = joint + product(k, u)
        column = column + jnp.sum(joint.reshape(STRIPE // 8, 8, G), axis=0)
        if k:
            fx, p, fl = k // 8, k // 2 % 4, k % 2
            rs_out[rows] = joint.astype(jnp.bfloat16)
            rs_copies[k] = remote(
                rs_out.at[rows], rs_in.at[k], rs_send.at[k], rs_recv.at[k], dev(fx=fx, dy=REL_Y[p], fl=fl))
            if not PRIOR_FIRST:
                go(rs_copies[k])
        else:
            acc[rows] = joint

    here = (y * 2 + xl) * 2 + xh

    def reduce_over(value, peers, index, out, box, send, recv):
        out[...] = value
        box[index] = value
        copies = [go(remote(out, box.at[index], send.at[i], recv.at[i], peer)) for i, peer in enumerate(peers)]
        return copies

    plane_devices = [dev(fx=fx, dy=dy, fl=fl) for fx, dy, fl in plane]
    line_devices = [dev(dz=dz, fq=fq) for dz, fq in line]
    column = jnp.sum(column, axis=0, keepdims=True)
    if PRIOR_FIRST:
        copies = reduce_over(column, plane_devices, here, pr_out, pr_in, pr_send, pr_recv)
        for k in ORDER:
            if k:
                go(rs_copies[k])
        for copy in copies:
            copy.wait_recv()
        copies = reduce_over(jnp.sum(pr_in[...], axis=0), line_devices, me, pr2_out, pr2_in, pr2_send, pr2_recv)
    else:
        copies = reduce_over(column, line_devices, me, pr2_out, pr2_in, pr2_send, pr2_recv)
        for copy in copies:
            copy.wait_recv()
        copies = reduce_over(jnp.sum(pr2_in[...], axis=0), plane_devices, here, pr_out, pr_in, pr_send, pr_recv)

    total = acc[0:STRIPE]
    for k in ORDER:
        if k:
            rs_copies[k].wait_recv()
            total = total + rs_in[k].astype(jnp.float32)
    for copy in copies:
        copy.wait_recv()
    prior = jnp.sum((pr2_in if PRIOR_FIRST else pr_in)[...], axis=0) / DOCS
    joint = total / DOCS
    cluster_mass = jnp.sum(joint, axis=1, keepdims=True)
    lift = joint / (cluster_mass * prior)
    lift_ref[...] = lift
    information = jnp.sum((joint * jnp.log(lift)).reshape(STRIPE // 8, 8, G), axis=0)
    information = jnp.sum(information, axis=0, keepdims=True)

    copies = reduce_over(information, line_devices, me, in_out, in_in, in_send, in_recv)
    for copy in copies:
        copy.wait_recv()
    copies = reduce_over(jnp.sum(in_in[...], axis=0), plane_devices, here, in2_out, in2_in, in2_send, in2_recv)
    for copy in copies:
        copy.wait_recv()
    info_ref[...] = jnp.sum(jnp.sum(in2_in[...], axis=0), axis=1, keepdims=True)
    for copy in sends:
        copy.wait_send()


def shards(documents, centroids, domain_mass):
    bf16, f32 = jnp.bfloat16, jnp.float32
    dma = pltpu.SemaphoreType.DMA
    vmem = pltpu.VMEM
    lift, information = pl.pallas_call(
        kernel,
        out_shape=(jax.ShapeDtypeStruct((STRIPE, G), f32), jax.ShapeDtypeStruct((1, 1), f32)),
        in_specs=[pl.BlockSpec(memory_space=pl.ANY)] * 3,
        out_specs=(pl.BlockSpec(memory_space=pltpu.VMEM), pl.BlockSpec(memory_space=pltpu.VMEM)),
        scratch_shapes=[
            vmem((NU, CH, E), bf16),
            vmem((ROWS, E), bf16),
            vmem((ROWS, E), bf16),
            vmem((HALF, G), f32),
            vmem((2, HALF, G), bf16),
            vmem((NU, 2 * ROWS, CH), f32),
            vmem((NU, 8, CH), f32),
            vmem((8, NU, 2, CH), f32),
            vmem((2 * ROWS, G), f32),
            vmem((2 * ROWS, G), bf16),
            vmem((16, STRIPE, G), bf16),
            vmem((1, G), f32),
            vmem((16, 1, G), f32),
            vmem((1, G), f32),
            vmem((8, 1, G), f32),
            vmem((1, G), f32),
            vmem((8, 1, G), f32),
            vmem((1, G), f32),
            vmem((16, 1, G), f32),
            dma((1 + NJ + 8,)),
            dma((NJ,)), dma((NJ,)),
            dma((NJ, 3)), dma((NJ, 3)), dma((NJ, 2)), dma((NJ, 2)),
            dma((NJ, 3)), dma((NJ, 3)), dma((NJ, 2)), dma((NJ, 2)),
            dma((NJ,)), dma((NJ,)),
            dma((NB // 2 + NB,)), dma((NB // 2 + NB,)),
            dma((NB // 2,)), dma((NB // 2,)),
            dma((NB, 3)), dma((NB, 3)),
            dma, dma,
            dma((2, 7)), dma((2, 7)),
            dma((16,)), dma((16,)),
            dma((15,)), dma((15,)),
            dma((7,)), dma((7,)),
            dma((7,)), dma((7,)),
            dma((15,)), dma((15,)),
        ],
        compiler_params=pltpu.CompilerParams(
            collective_id=0, has_side_effects=True, vmem_limit_bytes=56 << 20),
    )(documents, centroids, domain_mass)
    return lift, information.reshape(())


def solution(mesh):
    return jax.shard_map(
        shards,
        mesh=mesh,
        in_specs=(P("dp", "cluster"), P("cluster", None), P("dp", None)),
        out_specs=(P(("cluster", "dp"), None), P()),
        check_vma=False,
    )
```

time: 94.3 us -> 80 us (0.85)
  Pallas kernels: 90.1 us -> 75.9 us
    pallas_call x1, Pallas kernels: 90.1 us -> 75.9 us  [shards(): pl.pallas_call(kernel, out_shape=(jax.ShapeDtypeStruct((STRIPE, G), f32),...]
where the time goes in v2:
time: 80 us; the launch traced here: 79.9 us
  Pallas kernels  75.9 us (95%)
  between operations  2.45 us (3%)
  local copies, waits for them, and re-layouts  1.57 us (2%)
    pallas_call x1, Pallas kernels, shards(): pl.pallas_call(kernel, out_shape=(jax.ShapeDtypeStruct((STRIPE, G), f32),...  75.9 us

profile of v2, /device:TPU:1, one launch (start us, length us, event | category | flops | bytes accessed | tf_op | source)
XLA Modules:
  0.0 79.9 jit_solution(3163163613707708704)
XLA Ops:
  0.6 75.9 %shard_map.50 = (f32[128,256]{1,0:T(8,128)}, f32[1,1]{1,0:T(1,128)}) custom-call(bf16[2048,128]{1,0:T(8,128)(2,1)} %docs_hbm.1, bf16[2048,1024]{1,0:T(8,128)(2,1)} %cent_hbm.1, f32[2048,256]{1,0:T(8,128)} %mass_hbm.1), custom_call_target="tpu_custom_call" | custom-call | tf_op jit(solution)/shard_map/pallas_call | solution.py:387
  76.5 1.6 %copy.7 = f32[128,256]{1,0:T(8,128)} copy(f32[128,256]{1,0:T(8,128)} %get-tuple-element.8) | data formatting | bytes 262144

commit v3 on v2

--- a/solution.py
+++ b/solution.py
@@ -22,11 +22,12 @@
 WAYS = (1, 3, 2)
 ZN, FN, ZW = 2, 3, 4
 PRIOR_FIRST = True
+SETTLE, EARLY_OUT, NEAR = True, True, True
 SCHEDULE = (
-    "x0", "b0", "z0", "x1", "b1", "z1", "x2", "b2", "z2", "x3", "b3", "z3",
-    "l0", "D0,1,2,3,4,5,6,7", "l1", "L", "c0", "l2", "l3", "p0,0", "s0", "p1,0", "c1", "p2,0",
-    "s1", "p3,0", "a0,4", "P0,4,1", "c2", "a4,8", "P0,4,2", "P0,4,3", "w4", "s2", "c3", "w5",
-    "t0", "w6", "s3", "w7", "t1",
+    "x0", "b0", "D0,1,2,3,4,5,6,7", "z0", "x1", "b1", "z1", "x2", "b2", "z2", "x3", "b3",
+    "z3", "l0", "l1", "L", "c0", "l2", "l3", "p0,0", "s0", "p1,0", "c1", "p2,0",
+    "s1", "p3,0", "a0,4", "P0,4,1", "c2", "p4,0", "p4,1", "a4,8", "P0,4,2", "P0,4,3", "s2", "c3",
+    "p4,2", "p4,3", "w5", "t0", "w6", "s3", "w7", "t1",
 )
 XW, BW = 4, 4
 BATCHES = ((0, 6), (6, 8))
@@ -38,8 +39,9 @@
 EXP2_SCALE = 3.0 / math.sqrt(E) * math.log2(math.e)
 REL_Y = (0, 1, 3, 2)
 SLOT = {rel: p for p, rel in enumerate(REL_Y)}
-SETS = ((0, 1024), (1024, 512), (1536, 256), (1792, 256))
-NS = len(SETS)
+SETS = ((0, 4), (4, 6), (6, 7), (7, 8))
+BLOCK = 256
+NS = 8
 
 
 def kernel(docs_hbm, cent_hbm, mass_hbm, lift_ref, info_ref,
@@ -47,7 +49,7 @@
            rs_out, rs_in, pr_out, pr_in, pr2_out, pr2_in, in_out, in_in, in2_out, in2_in,
            load_sem, x_send, x_recv, z_send, z_recv, zz_send, zz_recv, f_send, f_recv, ff_send, ff_recv, s_send, s_recv,
            b_send, b_recv, l_send, l_recv, y_send, y_recv, h_send, h_recv, st_send, st_recv,
-           rs_send, rs_recv, pr_send, pr_recv, pr2_send, pr2_recv, in_send, in_recv, in2_send, in2_recv):
+           rs_send, rs_recv, pr_send, pr_recv, pr2_send, pr2_recv, in_send, in_recv, in2_send, in2_recv, lift_vmem, lift_sem):
     c = lax.axis_index("cluster")
     d = lax.axis_index("dp")
     z, xh = c // 2, lax.rem(c, 2)
@@ -70,10 +72,10 @@
             device_id=device, device_id_type=MESH)
 
     barrier = pltpu.get_barrier_semaphore()
-    for dz, fq in line:
-        pl.semaphore_signal(barrier, inc=1, device_id=dev(dz=dz, fq=fq), device_id_type=MESH)
-    for fx, dy, fl in plane:
-        pl.semaphore_signal(barrier, inc=1, device_id=dev(fx=fx, dy=dy, fl=fl), device_id_type=MESH)
+    near = [dict(dz=dz, fq=fq) for dz, fq in line if not (NEAR and dz and fq)]
+    near += [dict(fx=fx, dy=dy, fl=fl) for fx, dy, fl in plane if not (NEAR and dy and (fx or fl))]
+    for peer in near:
+        pl.semaphore_signal(barrier, inc=1, device_id=dev(**peer), device_id_type=MESH)
 
     def cols(cc):
         return pl.ds(pl.multiple_of(cc * 128, 128), 128)
@@ -95,7 +97,7 @@
     for copy in loads:
         copy.start()
     loads[0].wait()
-    pl.semaphore_wait(barrier, len(line) + len(plane))
+    pl.semaphore_wait(barrier, len(near))
 
     sends = []
 
@@ -188,27 +190,16 @@
         along_y(2 * i + 1)
 
     def part(u, s):
-        start, count = SETS[s] if s is not None else (0, 2 * ROWS)
         block_docs = docs[u]
-        top = jnp.full((8, CH), -jnp.inf, jnp.float32)
-        for r in range(start, start + count, 256):
-            block = own_c[r:r + 256] if r < ROWS else far_c[r - ROWS:r - ROWS + 256]
+        for n in range(*(SETS[s] if s is not None else (0, NS))):
+            r = n * BLOCK
+            block = own_c[r:r + BLOCK] if r < ROWS else far_c[r - ROWS:r - ROWS + BLOCK]
             raw = lax.dot_general(block, block_docs, NT, preferred_element_type=jnp.float32)
-            expo[u, r:r + 256] = raw
-            top = jnp.maximum(top, jnp.max(raw.reshape(32, 8, CH), axis=0))
-        top = jnp.max(top, axis=0, keepdims=True)
-        total = jnp.zeros((8, CH), jnp.float32)
-        for r in range(start, start + count, 256):
-            value = jnp.exp2((expo[u, r:r + 256] - top) * EXP2_SCALE)
-            expo[u, r:r + 256] = value
-            total = total + jnp.sum(value.reshape(32, 8, CH), axis=0)
-        total = jnp.sum(total, axis=0, keepdims=True)
-        if s is None:
-            setstat[u, 0:NS] = jnp.broadcast_to(top, (NS, CH))
-            setstat[u, NS:2 * NS] = jnp.concatenate([total, jnp.zeros((NS - 1, CH), jnp.float32)], axis=0)
-        else:
-            setstat[u, s:s + 1] = top
-            setstat[u, NS + s:NS + s + 1] = total
+            top = jnp.max(raw, axis=0, keepdims=True)
+            value = jnp.exp2((raw - top) * EXP2_SCALE)
+            expo[u, r:r + BLOCK] = value
+            setstat[u, n:n + 1] = top
+            setstat[u, NS + n:NS + n + 1] = jnp.sum(value, axis=0, keepdims=True)
 
     s_copies = []
 
@@ -288,13 +279,13 @@
 
     def product(k, u):
         if k < 8:
-            assign = expo[u, k * STRIPE:(k + 1) * STRIPE] * setstat[u, 0:1]
+            assign = expo[u, k * STRIPE:(k + 1) * STRIPE] * setstat[u, k // 2:k // 2 + 1]
         else:
             p, fl = k // 2 % 4, k % 2
             rows = []
             for i in range(fl, NB, 2):
                 r = ROWS + (4 * i + p) * PIECE
-                s = [n for n, (start, count) in enumerate(SETS) if start <= r < start + count][0]
+                s = r // BLOCK
                 rows.append(expo[u, r:r + PIECE] * setstat[u, s:s + 1])
             assign = jnp.concatenate(rows, axis=0)
         return jnp.dot(assign.astype(jnp.bfloat16), shares[u % 2, u // 2 * CH:(u // 2 + 1) * CH],
@@ -354,6 +345,13 @@
             copy.wait_recv()
         copies = reduce_over(jnp.sum(pr2_in[...], axis=0), plane_devices, here, pr_out, pr_in, pr_send, pr_recv)
 
+    def settle():
+        for copy in sends:
+            copy.wait_send()
+        sends.clear()
+
+    if SETTLE:
+        settle()
     total = acc[0:STRIPE]
     for k in ORDER:
         if k:
@@ -365,7 +363,12 @@
     joint = total / DOCS
     cluster_mass = jnp.sum(joint, axis=1, keepdims=True)
     lift = joint / (cluster_mass * prior)
-    lift_ref[...] = lift
+    if EARLY_OUT:
+        lift_vmem[...] = lift
+        lift_copy = pltpu.make_async_copy(lift_vmem, lift_ref, lift_sem)
+        lift_copy.start()
+    else:
+        lift_ref[...] = lift
     information = jnp.sum((joint * jnp.log(lift)).reshape(STRIPE // 8, 8, G), axis=0)
     information = jnp.sum(information, axis=0, keepdims=True)
 
@@ -376,8 +379,9 @@
     for copy in copies:
         copy.wait_recv()
     info_ref[...] = jnp.sum(jnp.sum(in2_in[...], axis=0), axis=1, keepdims=True)
-    for copy in sends:
-        copy.wait_send()
+    settle()
+    if EARLY_OUT:
+        lift_copy.wait()
 
 
 def shards(documents, centroids, domain_mass):
@@ -388,7 +392,7 @@
         kernel,
         out_shape=(jax.ShapeDtypeStruct((STRIPE, G), f32), jax.ShapeDtypeStruct((1, 1), f32)),
         in_specs=[pl.BlockSpec(memory_space=pl.ANY)] * 3,
-        out_specs=(pl.BlockSpec(memory_space=pltpu.VMEM), pl.BlockSpec(memory_space=pltpu.VMEM)),
+        out_specs=(pl.BlockSpec(memory_space=pl.ANY if EARLY_OUT else pltpu.VMEM), pl.BlockSpec(memory_space=pltpu.VMEM)),
         scratch_shapes=[
             vmem((NU, CH, E), bf16),
             vmem((ROWS, E), bf16),
@@ -396,7 +400,7 @@
             vmem((HALF, G), f32),
             vmem((2, HALF, G), bf16),
             vmem((NU, 2 * ROWS, CH), f32),
-            vmem((NU, 8, CH), f32),
+            vmem((NU, 2 * NS, CH), f32),
             vmem((8, NU, 2, CH), f32),
             vmem((2 * ROWS, G), f32),
             vmem((2 * ROWS, G), bf16),
@@ -424,6 +428,8 @@
             dma((7,)), dma((7,)),
             dma((7,)), dma((7,)),
             dma((15,)), dma((15,)),
+            vmem((STRIPE, G), f32),
+            dma,
         ],
         compiler_params=pltpu.CompilerParams(
             collective_id=0, has_side_effects=True, vmem_limit_bytes=56 << 20),

time: 80 us -> 76.8 us (0.960)
  Pallas kernels: 75.9 us -> 72.7 us
    pallas_call x1, Pallas kernels: 75.9 us -> 72.7 us  [shards(): pl.pallas_call(kernel, out_shape=(jax.ShapeDtypeStruct((STRIPE, G), f32),...]
where the time goes in v3:
time: 76.8 us; the launch traced here: 76.7 us
  Pallas kernels  72.7 us (95%)
  between operations  2.45 us (3%)
  local copies, waits for them, and re-layouts  1.57 us (2%)
    pallas_call x1, Pallas kernels, shards(): pl.pallas_call(kernel, out_shape=(jax.ShapeDtypeStruct((STRIPE, G), f32),...  72.7 us
    unnamed x1, local copies, waits for them, and re-layouts  1.57 us

profile of v3, /device:TPU:1, one launch (start us, length us, event | category | flops | bytes accessed | tf_op | source)
XLA Modules:
  0.0 76.7 jit_solution(16305022484141511436)
XLA Ops:
  0.6 72.7 %shard_map.50 = (f32[128,256]{1,0:T(8,128)}, f32[1,1]{1,0:T(1,128)}) custom-call(bf16[2048,128]{1,0:T(8,128)(2,1)} %docs_hbm.1, bf16[2048,1024]{1,0:T(8,128)(2,1)} %cent_hbm.1, f32[2048,256]{1,0:T(8,128)} %mass_hbm.1), custom_call_target="tpu_custom_call" | custom-call | tf_op jit(solution)/shard_map/pallas_call | solution.py:391
  73.3 1.6 %copy.7 = f32[128,256]{1,0:T(8,128)} copy(f32[128,256]{1,0:T(8,128)} %get-tuple-element.8) | data formatting | bytes 262144

commit v4 on v3

--- a/solution.py
+++ b/solution.py
@@ -24,7 +24,7 @@
 PRIOR_FIRST = True
 SETTLE, EARLY_OUT, NEAR = True, True, True
 SCHEDULE = (
-    "x0", "b0", "D0,1,2,3,4,5,6,7", "z0", "x1", "b1", "z1", "x2", "b2", "z2", "x3", "b3",
+    "D0,1,2,3,4,5,6,7", "x0", "b0", "z0", "x1", "b1", "z1", "x2", "b2", "z2", "x3", "b3",
     "z3", "l0", "l1", "L", "c0", "l2", "l3", "p0,0", "s0", "p1,0", "c1", "p2,0",
     "s1", "p3,0", "a0,4", "P0,4,1", "c2", "p4,0", "p4,1", "a4,8", "P0,4,2", "P0,4,3", "s2", "c3",
     "p4,2", "p4,3", "w5", "t0", "w6", "s3", "w7", "t1",
@@ -277,28 +277,29 @@
             total = jnp.sum(totals * jnp.exp2((tops - top) * EXP2_SCALE), axis=0, keepdims=True)
             setstat[u, 0:NS] = jnp.exp2((setstat[u, 0:NS] - top) * EXP2_SCALE) / total
 
-    def product(k, u):
+    def assigned(k, u):
         if k < 8:
-            assign = expo[u, k * STRIPE:(k + 1) * STRIPE] * setstat[u, k // 2:k // 2 + 1]
-        else:
-            p, fl = k // 2 % 4, k % 2
-            rows = []
-            for i in range(fl, NB, 2):
-                r = ROWS + (4 * i + p) * PIECE
-                s = r // BLOCK
-                rows.append(expo[u, r:r + PIECE] * setstat[u, s:s + 1])
-            assign = jnp.concatenate(rows, axis=0)
-        return jnp.dot(assign.astype(jnp.bfloat16), shares[u % 2, u // 2 * CH:(u // 2 + 1) * CH],
-                       preferred_element_type=jnp.float32)
+            return (expo[u, k * STRIPE:(k + 1) * STRIPE] * setstat[u, k // 2:k // 2 + 1]).astype(jnp.bfloat16)
+        p, fl = k // 2 % 4, k % 2
+        rows = []
+        for i in range(fl, NB, 2):
+            r = ROWS + (4 * i + p) * PIECE
+            rows.append(expo[u, r:r + PIECE] * setstat[u, r // BLOCK:r // BLOCK + 1])
+        return jnp.concatenate(rows, axis=0).astype(jnp.bfloat16)
+
+    def product(k, first, last):
+        total = None
+        for side in range(2):
+            assign = jnp.concatenate([assigned(k, u) for u in range(first + side, last, 2)], axis=1)
+            term = jnp.dot(assign, shares[side, first // 2 * CH:last // 2 * CH], preferred_element_type=jnp.float32)
+            total = term if total is None else total + term
+        return total
 
     h_copy.wait_recv()
     factors(0)
 
     for k in range(16):
-        joint = product(k, 0)
-        for u in range(1, EARLY):
-            joint = joint + product(k, u)
-        acc[k * STRIPE:(k + 1) * STRIPE] = joint
+        acc[k * STRIPE:(k + 1) * STRIPE] = product(k, 0, EARLY)
 
     factors(1)
 
@@ -306,9 +307,7 @@
     column = jnp.zeros((8, G), jnp.float32)
     for k in ORDER:
         rows = pl.ds(k * STRIPE, STRIPE)
-        joint = acc[rows]
-        for u in range(EARLY, NU):
-            joint = joint + product(k, u)
+        joint = acc[rows] + product(k, EARLY, NU)
         column = column + jnp.sum(joint.reshape(STRIPE // 8, 8, G), axis=0)
         if k:
             fx, p, fl = k // 8, k // 2 % 4, k % 2

time: 76.8 us -> 76.9 us (level)
  no operation moved by 1% of the time
where the time goes in v4:
time: 76.9 us; the launch traced here: 76.7 us
  Pallas kernels  72.7 us (95%)
  between operations  2.45 us (3%)
  local copies, waits for them, and re-layouts  1.57 us (2%)
    pallas_call x1, Pallas kernels, shards(): pl.pallas_call(kernel, out_shape=(jax.ShapeDtypeStruct((STRIPE, G), f32),...  72.7 us
    unnamed x1, local copies, waits for them, and re-layouts  1.57 us

profile of v4, /device:TPU:1, one launch (start us, length us, event | category | flops | bytes accessed | tf_op | source)
XLA Modules:
  0.0 76.7 jit_solution(7624910295060553853)
XLA Ops:
  0.6 72.7 %shard_map.50 = (f32[128,256]{1,0:T(8,128)}, f32[1,1]{1,0:T(1,128)}) custom-call(bf16[2048,128]{1,0:T(8,128)(2,1)} %docs_hbm.1, bf16[2048,1024]{1,0:T(8,128)(2,1)} %cent_hbm.1, f32[2048,256]{1,0:T(8,128)} %mass_hbm.1), custom_call_target="tpu_custom_call" | custom-call | tf_op jit(solution)/shard_map/pallas_call | solution.py:390
  73.3 1.6 %copy.7 = f32[128,256]{1,0:T(8,128)} copy(f32[128,256]{1,0:T(8,128)} %get-tuple-element.8) | data formatting | bytes 262144
